TPU v7x, 32 devices: a whole 2x2x4 slice. The times are simulated.
32 devices in a mesh: groups: 2 (over y), pair: 4 (over z), ri: 2 (over x), rep: 2 (over core).
Axes of the slice: x: 2, y: 2, z: 4, core: 2. Of those that a mesh axis runs over, the one named last changes fastest.
Arguments:
- b_int: bfloat16 [16, 12, 128, 640], P(('groups', 'ri'), None, 'pair'), parts along dimension 0, may hold values from -0.1875 to 0.1875
- gv_band: bfloat16 [24, 128, 1664], P(('groups', 'pair')), parts along dimension 0, may hold values from -0.25 to 0.25
- go_band: bfloat16 [24, 128, 640], P(('groups', 'pair'), 'rep'), parts along dimension 0, may hold values from -0.25 to 0.25
- mask: int32 [24, 5], P('groups'), parts along dimension 0, may hold values from 0 to 1, as said below
Outputs:
- chi: float32 [16, 8], P(('groups', 'ri')), parts along dimension 0
There are 2 independent parts, one for each index of `groups`. A program takes and returns all parts, laid end to end along the dimension named above; each array names one. Nothing has to cross between parts.
Inputs may be any that keep to these rules, and one draw needn't show every extreme that they name: mask[I, 2] is 1 for every block I.
All inputs are finite; a program needn't handle non-finite values.
Results may differ from a plain program's by a relative error of at most 0.0045.
Values may be sent and summed in bfloat16 or wider, within the bound.
A program may use at most 64 MiB of HBM per device.

v0:
```python
import jax
import jax.numpy as jnp
from jax import lax
from jax.sharding import PartitionSpec as P

BS = 128
R = 2


def with_halo(array, sides, width):
    for axis, dim in sides:
        size, length = (lax.axis_size(axis), array.shape[dim])
        up = [(i, (i + 1) % size) for i in range(size)]
        down = [(j, i) for i, j in up]
        last = lax.slice_in_dim(array, length - width, length, axis=dim)
        initial = lax.slice_in_dim(array, 0, width, axis=dim)
        before = lax.ppermute(last, axis, up)
        after = lax.ppermute(initial, axis, down)
        array = jnp.concatenate([before, array, after], axis=dim)
    return array


def per_device(b_int, gv_band, go_band, mask):
    local = lax.all_to_all(b_int, "pair", split_axis=1, concat_axis=2, tiled=True)
    ri_count = local.shape[0]
    blocks_here = local.shape[1]
    neighbours = 2 * R + 1
    window = 4 * R + 1
    first_block = lax.axis_index("pair") * blocks_here
    own_mask = lax.dynamic_slice_in_dim(mask, first_block, blocks_here, 0)
    shaped = local.reshape(ri_count, blocks_here, BS, neighbours, BS)
    masked = (shaped * own_mask.astype(jnp.bfloat16)[None, :, None, :, None]).reshape(
        ri_count, blocks_here, BS, neighbours * BS
    )
    wide_three = with_halo(masked, (("pair", 1),), R)
    wide_virtual = with_halo(gv_band, (("pair", 0),), R)
    half_rows = go_band.shape[1]
    row_start = lax.axis_index("rep") * half_rows
    own_rows = lax.dynamic_slice_in_dim(masked, row_start, half_rows, 2)
    x_acc = jnp.zeros((ri_count, blocks_here, half_rows, window * BS), jnp.float32)
    y_acc = jnp.zeros((ri_count, blocks_here, half_rows, window * BS), jnp.float32)
    for offset in range(neighbours):
        x_acc = x_acc + jnp.einsum(
            "pimn,inc->pimc",
            own_rows[..., offset * BS : (offset + 1) * BS],
            wide_virtual[
                offset : offset + blocks_here, :, (2 * R - offset) * BS : (6 * R - offset + 1) * BS
            ],
            preferred_element_type=jnp.float32,
        )
        neighbour_rows = wide_three[:, offset : offset + blocks_here]
        part_y = jnp.einsum(
            "iml,qilc->qimc",
            go_band[:, :, offset * BS : (offset + 1) * BS],
            neighbour_rows,
            preferred_element_type=jnp.float32,
        )
        y_acc = y_acc.at[..., offset * BS : (offset + neighbours) * BS].add(part_y)
    x_flat = x_acc.astype(jnp.bfloat16).reshape(ri_count, -1)
    y_flat = y_acc.astype(jnp.bfloat16).reshape(ri_count, -1)
    product = jnp.einsum(
        "pk,qk->pq",
        x_flat,
        lax.all_gather(y_flat, "ri", axis=0, tiled=True),
        preferred_element_type=jnp.float32,
    )
    return lax.psum(product, ("pair", "rep"))


def solution(mesh):
    in_specs = (
        P(("groups", "ri"), None, "pair", None),
        P(("groups", "pair"), None, None),
        P(("groups", "pair"), "rep", None),
        P("groups", None),
    )
    out_specs = P(("groups", "ri"), None)
    return jax.shard_map(
        per_device, mesh=mesh, in_specs=in_specs, out_specs=out_specs, check_vma=False
    )
```

profile of v0, /device:TPU:0, one launch (start us, length us, event | category | flops | bytes accessed | tf_op | source)
XLA Modules:
  0.0 212.3 jit_solution(16822826625087529878)
XLA Ops:
  6.5 3.1 %copy.11 = bf16[4,12,32,640]{3,2,0,1:T(8,128)(2,1)} copy(bf16[4,12,32,640]{3,2,1,0:T(8,128)(2,1)} %param.14) | data formatting | bytes 3932160 | tf_op args[0]
  9.7 6.4 %all-to-all-start = ((bf16[4,12,32,640]{3,2,0,1:T(8,128)(2,1)}), bf16[4,12,32,640]{3,2,0,1:T(8,128)(2,1)S(1)}, u32[]{:S(2)}, u32[]{:S(2)}) async-start(bf16[4,12,32,640]{3,2,0,1:T(8,128)(2,1)} %copy.11), calls=%async_computation | async-start | bytes 3932160 | tf_op jit(solution)/shard_map/all_to_all | solution.py:24
  16.4 45.1 %all-to-all-done = bf16[4,12,32,640]{3,2,0,1:T(8,128)(2,1)S(1)} async-done(((bf16[4,12,32,640]{3,2,0,1:T(8,128)(2,1)}), bf16[4,12,32,640]{3,2,0,1:T(8,128)(2,1)S(1)}, u32[]{:S(2)}, u32[]{:S(2)}) %all-to-all-start) | async-done | bytes 1966112 | tf_op jit(solution)/shard_map/all_to_all | solution.py:24
  62.6 3.8 %collective-permute-start.3 = (bf16[4,2,128,640]{3,2,0,1:T(8,128)(2,1)S(1)}, bf16[4,2,128,640]{3,2,0,1:T(8,128)(2,1)S(1)}, u32[]{:S(2)}, u32[]{:S(2)}) collective-permute-start(bf16[4,2,128,640]{3,2,0,1:T(8,128)(2,1)S(1)} %get-tuple-element.65), channel_id=1, source_target_pairs={{4,0},{8,4},{12,8},{0,12},{5,1},{9,5},{13,9},{1,13},{6,2},{10,6},{... | collective-permute-start | bytes 3932168 | tf_op jit(solution)/shard_map/ppermute | solution.py:18
  66.4 1.3 fusion.52
  67.8 28.3 %collective-permute-done.2 = bf16[4,2,128,640]{3,2,0,1:T(8,128)(2,1)S(1)} collective-permute-done((bf16[4,2,128,640]{3,2,0,1:T(8,128)(2,1)S(1)}, bf16[4,2,128,640]{3,2,0,1:T(8,128)(2,1)S(1)}, u32[]{:S(2)}, u32[]{:S(2)}) %collective-permute-start.2) | collective-permute-done | bytes 1310752 | tf_op jit(solution)/shard_map/ppermute | solution.py:17
  96.9 0.7 fusion.18
  97.6 0.7 fusion.15
  98.3 22.3 %collective-permute-done.3 = bf16[4,2,128,640]{3,2,0,1:T(8,128)(2,1)S(1)} collective-permute-done((bf16[4,2,128,640]{3,2,0,1:T(8,128)(2,1)S(1)}, bf16[4,2,128,640]{3,2,0,1:T(8,128)(2,1)S(1)}, u32[]{:S(2)}, u32[]{:S(2)}) %collective-permute-start.3) | collective-permute-done | bytes 1310752 | tf_op jit(solution)/shard_map/ppermute | solution.py:18
  120.6 0.7 fusion.14
  121.4 0.7 fusion.13
  122.3 1.4 copy.15
  123.7 3.3 %reshape.186 = bf16[1,4,221184]{2,1,0:T(4,128)(2,1)} reshape(bf16[4,3,64,1152]{3,2,1,0:T(8,128)(2,1)} %copy.15) | data formatting | bytes 3538944
  127.1 5.3 %collective-permute-start.1 = (bf16[2,128,1664]{2,1,0:T(8,128)(2,1)}, bf16[2,128,1664]{2,1,0:T(8,128)(2,1)}, u32[]{:S(2)}, u32[]{:S(2)}) collective-permute-start(bf16[2,128,1664]{2,1,0:T(8,128)(2,1)} %get-tuple-element.70), channel_id=1, source_target_pairs={{4,0},{8,4},{12,8},{0,12},{5,1},{9,5},{13,9},{1,13},{6,2},{10,6},{... | collective-permute-start | bytes 2555912 | tf_op jit(solution)/shard_map/ppermute | solution.py:18
  132.3 10.3 %collective-permute-done = bf16[2,128,1664]{2,1,0:T(8,128)(2,1)} collective-permute-done((bf16[2,128,1664]{2,1,0:T(8,128)(2,1)}, bf16[2,128,1664]{2,1,0:T(8,128)(2,1)}, u32[]{:S(2)}, u32[]{:S(2)}) %collective-permute-start) | collective-permute-done | bytes 852000 | tf_op jit(solution)/shard_map/ppermute | solution.py:17
  142.6 1.2 constant_dynamic-update-slice_fusion.1
  144.1 14.8 %collective-permute-done.1 = bf16[2,128,1664]{2,1,0:T(8,128)(2,1)} collective-permute-done((bf16[2,128,1664]{2,1,0:T(8,128)(2,1)}, bf16[2,128,1664]{2,1,0:T(8,128)(2,1)}, u32[]{:S(2)}, u32[]{:S(2)}) %collective-permute-start.1) | collective-permute-done | bytes 852000 | tf_op jit(solution)/shard_map/ppermute | solution.py:18
  158.9 1.3 constant_dynamic-update-slice_fusion.2
  162.6 1.0 fusion.4
  163.8 2.7 %copy.27 = bf16[1,4,192,1152]{3,1,2,0:T(4,128)(2,1)} copy(bf16[1,4,192,1152]{3,2,1,0:T(8,128)(2,1)S(1)} %bitcast.97) | data formatting | bytes 3538944
  166.5 12.8 %all-gather.3.cloned.1.call-done = bf16[2,4,221184]{2,1,0:T(4,128)(2,1)} async-done(((bf16[1,4,221184]{2,1,0:T(4,128)(2,1)}), bf16[2,4,221184]{2,1,0:T(4,128)(2,1)}) %all-gather.3.cloned.1.call-update) | async-done | bytes 3538960 | tf_op jit(solution)/shard_map/all_gather | solution.py:64
  179.3 4.7 %reshape.187 = bf16[8,221184]{1,0:T(8,128)(2,1)} reshape(bf16[2,4,221184]{2,1,0:T(4,128)(2,1)} %all-gather.3.cloned.1.call-done) | data formatting | bytes 7077888
  183.9 4.6 %fusion.53 = f32[4,8]{1,0:T(4,128)S(1)} fusion(bf16[4,221184]{1,0:T(4,128)(2,1)S(1)} %bitcast.98, bf16[8,221184]{1,0:T(8,128)(2,1)} %reshape.187), kind=kOutput, calls=%fused_computation.73 | convolution fusion | flops 14155776 | bytes 5308544 | tf_op jit(solution)/shard_map/pk,qk->pq/dot_general | solution.py:61
  188.5 16.9 %psum.7 = f32[4,8]{1,0:T(4,128)} all-reduce(f32[4,8]{1,0:T(4,128)S(1)} %fusion.53), channel_id=1, replica_groups=mesh['groups'=2,'pair'=4,'ri'=2,'rep'=2] {'pair','rep'}, use_global_device_ids=true, to_apply=%region_0.0 | all-reduce | flops 32 | bytes 256 | tf_op jit(solution)/shard_map/psum | solution.py:67
  (28 shorter events, 5.2 us)
Async XLA Ops:
  9.7 6.5 %copy-start.3 = (s32[12,5]{0,1:T(8,128)S(1)}, s32[12,5]{0,1:T(8,128)}, u32[]{:S(2)}) copy-start(s32[12,5]{0,1:T(8,128)} %param.17) | copy-start | bytes 724
  9.7 51.8 %all-to-all-start = ((bf16[4,12,32,640]{3,2,0,1:T(8,128)(2,1)}), bf16[4,12,32,640]{3,2,0,1:T(8,128)(2,1)S(1)}, u32[]{:S(2)}, u32[]{:S(2)}) async-start(bf16[4,12,32,640]{3,2,0,1:T(8,128)(2,1)} %copy.11), calls=%async_computation | async-start | bytes 3932160 | tf_op jit(solution)/shard_map/all_to_all | solution.py:24
  16.1 163.1 %all-gather.3.cloned.1.call-start = ((), (), s32[]{:S(2)}) async-start(), calls=%async_computation.1 | async-start | bytes 5308416 | tf_op jit(solution)/shard_map/all_gather | solution.py:64
  62.1 4.3 %copy-start = (bf16[3,128,1664]{2,1,0:T(8,128)(2,1)S(1)}, bf16[3,128,1664]{2,1,0:T(8,128)(2,1)}, u32[]{:S(2)}) copy-start(bf16[3,128,1664]{2,1,0:T(8,128)(2,1)} %param.15) | copy-start | bytes 3833860
  62.5 33.6 %copy-start.2 = (bf16[3,64,640]{2,1,0:T(8,128)(2,1)S(1)}, bf16[3,64,640]{2,1,0:T(8,128)(2,1)}, u32[]{:S(2)}) copy-start(bf16[3,64,640]{2,1,0:T(8,128)(2,1)} %param.16) | copy-start | bytes 737284
  62.5 33.6 %collective-permute-start.2 = (bf16[4,2,128,640]{3,2,0,1:T(8,128)(2,1)S(1)}, bf16[4,2,128,640]{3,2,0,1:T(8,128)(2,1)S(1)}, u32[]{:S(2)}, u32[]{:S(2)}) collective-permute-start(bf16[4,2,128,640]{3,2,0,1:T(8,128)(2,1)S(1)} %get-tuple-element.66), channel_id=1, source_target_pairs={{0,4},{4,8},{8,12},{12,0},{1,5},{5,9},{9,13},{13,1},{2,6},{6,10},{... | collective-permute-start | bytes 3932168 | tf_op jit(solution)/shard_map/ppermute | solution.py:17
  62.6 58.0 %collective-permute-start.3 = (bf16[4,2,128,640]{3,2,0,1:T(8,128)(2,1)S(1)}, bf16[4,2,128,640]{3,2,0,1:T(8,128)(2,1)S(1)}, u32[]{:S(2)}, u32[]{:S(2)}) collective-permute-start(bf16[4,2,128,640]{3,2,0,1:T(8,128)(2,1)S(1)} %get-tuple-element.65), channel_id=1, source_target_pairs={{4,0},{8,4},{12,8},{0,12},{5,1},{9,5},{13,9},{1,13},{6,2},{10,6},{... | collective-permute-start | bytes 3932168 | tf_op jit(solution)/shard_map/ppermute | solution.py:18
  67.8 74.8 %collective-permute-start = (bf16[2,128,1664]{2,1,0:T(8,128)(2,1)}, bf16[2,128,1664]{2,1,0:T(8,128)(2,1)}, u32[]{:S(2)}, u32[]{:S(2)}) collective-permute-start(bf16[2,128,1664]{2,1,0:T(8,128)(2,1)} %get-tuple-element.69), channel_id=1, source_target_pairs={{0,4},{4,8},{8,12},{12,0},{1,5},{5,9},{9,13},{13,1},{2,6},{6,10},{... | collective-permute-start | bytes 2555912 | tf_op jit(solution)/shard_map/ppermute | solution.py:17
  127.1 31.8 %collective-permute-start.1 = (bf16[2,128,1664]{2,1,0:T(8,128)(2,1)}, bf16[2,128,1664]{2,1,0:T(8,128)(2,1)}, u32[]{:S(2)}, u32[]{:S(2)}) collective-permute-start(bf16[2,128,1664]{2,1,0:T(8,128)(2,1)} %get-tuple-element.70), channel_id=1, source_target_pairs={{4,0},{8,4},{12,8},{0,12},{5,1},{9,5},{13,9},{1,13},{6,2},{10,6},{... | collective-permute-start | bytes 2555912 | tf_op jit(solution)/shard_map/ppermute | solution.py:18
  166.5 17.4 %copy-start.1 = (bf16[1,4,192,1152]{3,1,2,0:T(4,128)(2,1)S(1)}, bf16[1,4,192,1152]{3,1,2,0:T(4,128)(2,1)}, u32[]{:S(2)}) copy-start(bf16[1,4,192,1152]{3,1,2,0:T(4,128)(2,1)} %copy.27) | copy-start | bytes 5308420
Sparse Core Ops, SparseCore 0:
  127.2 52.0 all-gather.2
where the time goes:
time: 213 us; the launch traced here: 212 us
  waiting for transfers between devices  134 us (63%)
  local copies, waits for them, and re-layouts  20.6 us (10%)
  blocking collectives  16.9 us (8%)
  starting transfers between devices  15.6 us (7%)
  between operations  13.5 us (6%)
  matrix products  11.3 us (5%)
    all_to_all x1, waiting for transfers between devices, per_device(): lax.all_to_all(b_int, 'pair', split_axis=1, concat_axis=2, tiled=True)  45.1 us
    ppermute x2, waiting for transfers between devices, with_halo(): before = lax.ppermute(last, axis, up)  38.6 us
    ppermute x2, waiting for transfers between devices, with_halo(): after = lax.ppermute(initial, axis, down)  37.1 us
    psum x1, blocking collectives, per_device(): return lax.psum(product, ('pair', 'rep'))  16.9 us
    unnamed x15, local copies, waits for them, and re-layouts  15.1 us
    all_gather x1, waiting for transfers between devices, per_device(): lax.all_gather(y_flat, 'ri', axis=0, tiled=True)  12.8 us
    ppermute x2, starting transfers between devices, with_halo(): after = lax.ppermute(initial, axis, down)  9.06 us
    all_to_all x1, starting transfers between devices, per_device(): lax.all_to_all(b_int, 'pair', split_axis=1, concat_axis=2, tiled=True)  6.45 us
  transfers between devices with their start and end apart: 6, of which 6 were waited for; matrix products, arithmetic and copies ran while one was open for 9% of the time, Pallas kernels for 0%

commit v1 on v0

--- a/solution.py
+++ b/solution.py
@@ -1,6 +1,10 @@
+import functools
+
 import jax
 import jax.numpy as jnp
 from jax import lax
+from jax.experimental import pallas as pl
+from jax.experimental.pallas import tpu as pltpu
 from jax.sharding import PartitionSpec as P
 
 BS = 128
@@ -67,6 +71,233 @@
     return lax.psum(product, ("pair", "rep"))
 
 
+WINDOW = 4 * R + 1
+NEAR = 2 * R + 1
+TRIM = WINDOW + 1
+VBAND = 6 * R + 1
+MESH = pl.DeviceIdType.MESH
+
+
+def remote(src, dst, send, recv, device):
+    return pltpu.make_async_remote_copy(
+        src_ref=src, dst_ref=dst, send_sem=send, recv_sem=recv, device_id=device, device_id_type=MESH
+    )
+
+
+def fused(
+    n, b_ref, gv_ref, go_ref, mask_ref, out_ref,
+    staged, three, halo, y_buf, x_buf, sums,
+    m_local, m_send, m_recv, f_send, f_recv, y_send, y_recv, g_send, g_recv, h_send, h_recv, c_send, c_recv,
+):
+    z, x, r = lax.axis_index("pair"), lax.axis_index("ri"), lax.axis_index("rep")
+    ri_here, nblk, rows, _ = b_ref.shape
+    nb = gv_ref.shape[0]
+    half = go_ref.shape[1]
+    carried = ri_here // 2
+    reach = nb + 2 * R
+    sibling = {"rep": 1 - r}
+    partner = {"ri": 1 - x}
+
+    barrier = pltpu.get_barrier_semaphore()
+    for d in range(n):
+        other = lax.rem(z + d, n)
+        if d:
+            pl.semaphore_signal(barrier, inc=1, device_id={"pair": other}, device_id_type=MESH)
+        pl.semaphore_signal(barrier, inc=1, device_id={"pair": other, "rep": 1 - r}, device_id_type=MESH)
+    pl.semaphore_signal(barrier, inc=1, device_id=partner, device_id_type=MESH)
+
+    for k in range(carried):
+        for block in range(nblk):
+            for o in range(NEAR):
+                cols = slice(o * BS, (o + 1) * BS)
+                present = mask_ref[block, o].astype(jnp.float32)
+                value = (b_ref[carried * r + k, block, :, cols].astype(jnp.float32) * present).astype(jnp.bfloat16)
+                staged[k, block, :, cols] = value
+                if block < reach - R:
+                    staged[k, block + nblk, :, cols] = value
+
+    pl.semaphore_wait(barrier, 2 * n)
+
+    def first(owner):
+        return lax.rem(owner * nb + nblk - R, nblk)
+
+    mine = pl.ds(pl.multiple_of(z * rows, rows), rows)
+    for k in range(carried):
+        q = carried * r + k
+        for d in range(1, n):
+            owner = lax.rem(z + d, n)
+            remote(
+                staged.at[k, pl.ds(first(owner), reach)], three.at[q, :, mine, :],
+                m_send.at[k], m_recv.at[k], {"pair": owner},
+            ).start()
+        pltpu.make_async_copy(
+            staged.at[k, pl.ds(first(z), reach)], three.at[q, :, mine, :], m_local.at[k]
+        ).start()
+
+    core_rows = pl.ds(pl.multiple_of(r * half, half), half)
+    before = slice((VBAND - TRIM) * BS, VBAND * BS)
+    after = slice(0, TRIM * BS)
+    up, down = {"pair": lax.rem(z + 1, n)}, {"pair": lax.rem(z + n - 1, n)}
+    virtual = [
+        (gv_ref.at[nb - R : nb, core_rows, before], halo.at[0:R, core_rows, before], up),
+        (gv_ref.at[0:R, core_rows, after], halo.at[R : 2 * R, core_rows, after], down),
+    ]
+    for s, (src, dst, device) in enumerate(virtual):
+        remote(src, dst, g_send.at[s], g_recv.at[s], device).start()
+
+    def occupied(q, slot):
+        for i in range(nb):
+            parts = [
+                jnp.dot(
+                    go_ref[i, :, o * BS : (o + 1) * BS], three[q, i + o], preferred_element_type=jnp.float32
+                )
+                for o in range(NEAR)
+            ]
+            for t in range(WINDOW):
+                total = None
+                for o in range(NEAR):
+                    if 0 <= t - o < NEAR:
+                        part = parts[o][:, (t - o) * BS : (t - o + 1) * BS]
+                        total = part if total is None else total + part
+                y_buf[0, i, q, :, t * BS : (t + 1) * BS] = total.astype(jnp.bfloat16)
+        remote(y_buf.at[0, :, q], y_buf.at[1, :, q], y_send.at[slot], y_recv.at[slot], partner).start()
+
+    for k in range(carried):
+        q = carried * r + k
+        theirs = carried * (1 - r) + k
+        pltpu.make_async_copy(
+            staged.at[k, pl.ds(first(z), reach)], three.at[q, :, mine, :], m_local.at[k]
+        ).wait()
+        others = three.at[q, :, 0 : (n - 1) * rows, :]
+        remote(others, others, m_send.at[k], m_recv.at[k], sibling).wait_recv()
+        remote(three.at[q], three.at[q], f_send.at[k], f_recv.at[k], sibling).start()
+        occupied(q, 2 * k)
+        remote(three.at[theirs], three.at[theirs], f_send.at[k], f_recv.at[k], sibling).wait_recv()
+        occupied(theirs, 2 * k + 1)
+
+    for s, (src, dst, device) in enumerate(virtual):
+        remote(dst, dst, g_send.at[s], g_recv.at[s], sibling).wait_recv()
+        remote(dst, dst, h_send.at[s], h_recv.at[s], sibling).start()
+    for s, (src, dst, device) in enumerate(virtual):
+        remote(dst, dst, h_send.at[s], h_recv.at[s], sibling).wait_recv()
+
+    def virtual_rows(j, cols):
+        if j < R:
+            return halo[j, :, cols]
+        if j < R + nb:
+            return gv_ref[j - R, :, cols]
+        return halo[j - nb, :, cols]
+
+    def products(side):
+        total = None
+        for i in range(nb):
+            part = lax.dot_general(
+                x_buf[i], y_buf[side, i].reshape(ri_here * half, WINDOW * BS),
+                (((1,), (1,)), ((), ())), preferred_element_type=jnp.float32,
+            )
+            total = part if total is None else total + part
+        return total
+
+    for i in range(nb):
+        total = None
+        for o in range(NEAR):
+            left = three[:, i + R, core_rows, o * BS : (o + 1) * BS].reshape(ri_here * half, BS)
+            part = jnp.dot(
+                left, virtual_rows(i + o, slice((2 * R - o) * BS, (6 * R - o + 1) * BS)),
+                preferred_element_type=jnp.float32,
+            )
+            total = part if total is None else total + part
+        x_buf[i] = total.astype(jnp.bfloat16)
+
+    size = ri_here * half
+    row_id = lax.broadcasted_iota(jnp.int32, (size, size), 0)
+    col_id = lax.broadcasted_iota(jnp.int32, (size, size), 1)
+    same = lax.rem(row_id, half) == lax.rem(col_id, half)
+    col_of = lax.broadcasted_iota(jnp.int32, (ri_here, size), 1) // half
+    lane = lax.broadcasted_iota(jnp.int32, (ri_here, BS), 1)
+    result = jnp.zeros((ri_here, BS), jnp.float32)
+    for side in range(2):
+        if side:
+            for slot in range(ri_here):
+                q = carried * (r if slot % 2 == 0 else 1 - r) + slot // 2
+                landed = y_buf.at[1, :, q]
+                remote(landed, landed, y_send.at[slot], y_recv.at[slot], partner).wait_recv()
+        diagonal = jnp.where(same, products(side), 0.0).reshape(ri_here, half, size).sum(axis=1)
+        base = ri_here * (x if side == 0 else 1 - x)
+        for q in range(ri_here):
+            value = jnp.sum(jnp.where(col_of == q, diagonal, 0.0), axis=1, keepdims=True)
+            result = jnp.where(lane == base + q, value, result)
+
+    slot = 2 * z + r
+    sums[slot, 0:ri_here, :] = result
+    for d in range(n):
+        other = lax.rem(z + d, n)
+        if d:
+            remote(sums.at[slot], sums.at[slot], c_send, c_recv, {"pair": other}).start()
+        remote(sums.at[slot], sums.at[slot], c_send, c_recv, {"pair": other, "rep": 1 - r}).start()
+    seven = sums.at[0 : 2 * n - 1]
+    remote(seven, seven, c_send, c_recv, sibling).wait_recv()
+    total = sums[0]
+    for s in range(1, 2 * n):
+        total = total + sums[s]
+    out_ref[...] = total[0:ri_here, 0 : 2 * ri_here]
+
+    remote(seven, seven, c_send, c_recv, sibling).wait_send()
+    for k in range(carried):
+        q = carried * r + k
+        others = three.at[q, :, 0 : (n - 1) * rows, :]
+        remote(others, others, m_send.at[k], m_recv.at[k], sibling).wait_send()
+        remote(three.at[q], three.at[q], f_send.at[k], f_recv.at[k], sibling).wait_send()
+    for slot in range(ri_here):
+        q = carried * (r if slot % 2 == 0 else 1 - r) + slot // 2
+        remote(y_buf.at[0, :, q], y_buf.at[0, :, q], y_send.at[slot], y_recv.at[slot], partner).wait_send()
+    for s, (src, dst, device) in enumerate(virtual):
+        remote(src, dst, g_send.at[s], g_recv.at[s], device).wait_send()
+        remote(dst, dst, h_send.at[s], h_recv.at[s], sibling).wait_send()
+
+
+def one_kernel(b_int, gv_band, go_band, mask):
+    n = lax.axis_size("pair")
+    ri_here, nblk, rows, width = b_int.shape
+    nb = gv_band.shape[0]
+    half = go_band.shape[1]
+    carried = ri_here // 2
+    reach = nb + 2 * R
+    dma = pltpu.SemaphoreType.DMA
+    vmem = pl.BlockSpec(memory_space=pltpu.VMEM)
+    return pl.pallas_call(
+        functools.partial(fused, n),
+        out_shape=jax.ShapeDtypeStruct((ri_here, 2 * ri_here), jnp.float32),
+        in_specs=[vmem, vmem, vmem, pl.BlockSpec(memory_space=pltpu.SMEM)],
+        out_specs=vmem,
+        scratch_shapes=[
+            pltpu.VMEM((carried, nblk + reach - R, rows, width), jnp.bfloat16),
+            pltpu.VMEM((ri_here, reach, BS, width), jnp.bfloat16),
+            pltpu.VMEM((2 * R, BS, gv_band.shape[2]), jnp.bfloat16),
+            pltpu.VMEM((2, nb, ri_here, half, WINDOW * BS), jnp.bfloat16),
+            pltpu.VMEM((nb, ri_here * half, WINDOW * BS), jnp.bfloat16),
+            pltpu.VMEM((2 * n, 8, BS), jnp.float32),
+            dma((carried,)), dma((carried,)), dma((carried,)), dma((carried,)), dma((carried,)),
+            dma((ri_here,)), dma((ri_here,)), dma((2,)), dma((2,)), dma((2,)), dma((2,)), dma, dma,
+        ],
+        compiler_params=pltpu.CompilerParams(
+            collective_id=0, has_side_effects=True, vmem_limit_bytes=40 * 1024 * 1024
+        ),
+    )(b_int, gv_band, go_band, mask)
+
+
+def on_device(b_int, gv_band, go_band, mask):
+    fits = (
+        lax.axis_size("ri") == 2
+        and lax.axis_size("rep") == 2
+        and b_int.shape[2] % 16 == 0
+        and b_int.shape[0] in (2, 4, 8)
+        and gv_band.shape[0] >= R
+        and gv_band.shape[0] + R <= b_int.shape[1]
+    )
+    return (one_kernel if fits else per_device)(b_int, gv_band, go_band, mask)
+
+
 def solution(mesh):
     in_specs = (
         P(("groups", "ri"), None, "pair", None),
@@ -76,5 +307,5 @@
     )
     out_specs = P(("groups", "ri"), None)
     return jax.shard_map(
-        per_device, mesh=mesh, in_specs=in_specs, out_specs=out_specs, check_vma=False
-    )
+        on_device, mesh=mesh, in_specs=in_specs, out_specs=out_specs, check_vma=False
+    )

time: 213 us -> 95.9 us (0.45)
  waiting for transfers between devices: 134 us -> 0 us
  Pallas kernels: 0 us -> 90.5 us
  blocking collectives: 16.9 us -> 0 us
  starting transfers between devices: 15.6 us -> 0 us
  local copies, waits for them, and re-layouts: 20.6 us -> 5.15 us
  between operations: 13.5 us -> 0.01 us
  matrix products: 11.3 us -> 0 us
    pallas_call x0 -> x1, Pallas kernels: none -> 90.5 us  [one_kernel(): pl.pallas_call(functools.partial(fused, n), out_shape=jax.ShapeDtypeStruc...]
    ppermute x4 -> x0, waiting for transfers between devices: 75.8 us -> none  [the longest x2 38.6 us: with_halo(): before = lax.ppermute(last, axis, up)]
    all_to_all x1 -> x0, waiting for transfers between devices: 45.1 us -> none  [per_device(): lax.all_to_all(b_int, 'pair', split_axis=1, concat_axis=2, tiled=True)]
    psum x1 -> x0, blocking collectives: 16.9 us -> none  [per_device(): return lax.psum(product, ('pair', 'rep'))]
    all_gather x1 -> x0, waiting for transfers between devices: 12.8 us -> none  [per_device(): lax.all_gather(y_flat, 'ri', axis=0, tiled=True)]
    dot_general x11 -> x0, matrix products: 11.3 us -> none  [the longest x1 4.59 us: per_device(): jnp.einsum('pk,qk->pq', x_flat, lax.all_gather(y_flat, 'ri', axis=0, tile...]
    unnamed x15 -> x8, local copies, waits for them, and re-layouts: 15.1 us -> 5.15 us
    ppermute x4 -> x0, starting transfers between devices: 9.12 us -> none  [the longest x2 9.06 us: with_halo(): after = lax.ppermute(initial, axis, down)]
  transfers between devices with their start and end apart: 6 -> 0, of which waited for: 6 -> 0; matrix products, arithmetic and copies ran while one was open for 9% -> 0% of each run, Pallas kernels for 0% -> 0%
where the time goes in v1:
time: 95.9 us; the launch traced here: 95.7 us
  Pallas kernels  90.5 us (94%)
  local copies, waits for them, and re-layouts  5.15 us (5%)
    pallas_call x1, Pallas kernels, one_kernel(): pl.pallas_call(functools.partial(fused, n), out_shape=jax.ShapeDtypeStruc...  90.5 us
    unnamed x8, local copies, waits for them, and re-layouts  5.15 us

profile of v1, /device:TPU:0, one launch (start us, length us, event | category | flops | bytes accessed | tf_op | source)
XLA Modules:
  0.0 95.7 jit_solution(3525574271671101011)
XLA Ops:
  0.0 0.8 copy.5.mask_ref
  0.8 0.0 copy-start
  0.8 1.5 %copy-done = bf16[4,12,32,640]{3,2,1,0:T(8,128)(2,1)S(1)} copy-done((bf16[4,12,32,640]{3,2,1,0:T(8,128)(2,1)S(1)}, bf16[4,12,32,640]{3,2,1,0:T(8,128)(2,1)}, u32[]{:S(2)}) %copy-start) | copy-done | bytes 1966104
  2.3 0.0 copy-start.1
  2.3 1.3 %copy-done.1 = bf16[3,128,1664]{2,1,0:T(8,128)(2,1)S(1)} copy-done((bf16[3,128,1664]{2,1,0:T(8,128)(2,1)S(1)}, bf16[3,128,1664]{2,1,0:T(8,128)(2,1)}, u32[]{:S(2)}) %copy-start.1) | copy-done | bytes 1277976
  3.6 0.0 copy-start.2
  3.6 0.9 copy-done.2
  4.6 90.5 %shard_map.46 = f32[4,8]{1,0:T(4,128)S(1)} custom-call(bf16[4,12,32,640]{3,2,1,0:T(8,128)(2,1)S(1)} %copy-done, bf16[3,128,1664]{2,1,0:T(8,128)(2,1)S(1)} %copy-done.1, bf16[3,64,640]{2,1,0:T(8,128)(2,1)S(1)} %copy-done.2, s32[12,5]{1,0:T(8,128)S(1)} %copy.5.mask_ref), custom_call_target="tpu_custom_call" | custom-call | tf_op jit(solution)/shard_map/pallas_call | solution.py:268
  95.1 0.6 copy.7
Async XLA Ops:
  0.8 1.5 %copy-start = (bf16[4,12,32,640]{3,2,1,0:T(8,128)(2,1)S(1)}, bf16[4,12,32,640]{3,2,1,0:T(8,128)(2,1)}, u32[]{:S(2)}) copy-start(bf16[4,12,32,640]{3,2,1,0:T(8,128)(2,1)} %b_ref.1) | copy-start | bytes 5898244
  2.3 1.3 %copy-start.1 = (bf16[3,128,1664]{2,1,0:T(8,128)(2,1)S(1)}, bf16[3,128,1664]{2,1,0:T(8,128)(2,1)}, u32[]{:S(2)}) copy-start(bf16[3,128,1664]{2,1,0:T(8,128)(2,1)} %gv_ref.1) | copy-start | bytes 3833860
  3.6 0.9 copy-start.2

commit v2 on v1

v2 whole, which is shorter than its diff:
```python
import functools

import jax
import jax.numpy as jnp
from jax import lax
from jax.experimental import pallas as pl
from jax.experimental.pallas import tpu as pltpu
from jax.sharding import PartitionSpec as P

BS = 128
R = 2


def with_halo(array, sides, width):
    for axis, dim in sides:
        size, length = (lax.axis_size(axis), array.shape[dim])
        up = [(i, (i + 1) % size) for i in range(size)]
        down = [(j, i) for i, j in up]
        last = lax.slice_in_dim(array, length - width, length, axis=dim)
        initial = lax.slice_in_dim(array, 0, width, axis=dim)
        before = lax.ppermute(last, axis, up)
        after = lax.ppermute(initial, axis, down)
        array = jnp.concatenate([before, array, after], axis=dim)
    return array


def per_device(b_int, gv_band, go_band, mask):
    local = lax.all_to_all(b_int, "pair", split_axis=1, concat_axis=2, tiled=True)
    ri_count = local.shape[0]
    blocks_here = local.shape[1]
    neighbours = 2 * R + 1
    window = 4 * R + 1
    first_block = lax.axis_index("pair") * blocks_here
    own_mask = lax.dynamic_slice_in_dim(mask, first_block, blocks_here, 0)
    shaped = local.reshape(ri_count, blocks_here, BS, neighbours, BS)
    masked = (shaped * own_mask.astype(jnp.bfloat16)[None, :, None, :, None]).reshape(
        ri_count, blocks_here, BS, neighbours * BS
    )
    wide_three = with_halo(masked, (("pair", 1),), R)
    wide_virtual = with_halo(gv_band, (("pair", 0),), R)
    half_rows = go_band.shape[1]
    row_start = lax.axis_index("rep") * half_rows
    own_rows = lax.dynamic_slice_in_dim(masked, row_start, half_rows, 2)
    x_acc = jnp.zeros((ri_count, blocks_here, half_rows, window * BS), jnp.float32)
    y_acc = jnp.zeros((ri_count, blocks_here, half_rows, window * BS), jnp.float32)
    for offset in range(neighbours):
        x_acc = x_acc + jnp.einsum(
            "pimn,inc->pimc",
            own_rows[..., offset * BS : (offset + 1) * BS],
            wide_virtual[
                offset : offset + blocks_here, :, (2 * R - offset) * BS : (6 * R - offset + 1) * BS
            ],
            preferred_element_type=jnp.float32,
        )
        neighbour_rows = wide_three[:, offset : offset + blocks_here]
        part_y = jnp.einsum(
            "iml,qilc->qimc",
            go_band[:, :, offset * BS : (offset + 1) * BS],
            neighbour_rows,
            preferred_element_type=jnp.float32,
        )
        y_acc = y_acc.at[..., offset * BS : (offset + neighbours) * BS].add(part_y)
    x_flat = x_acc.astype(jnp.bfloat16).reshape(ri_count, -1)
    y_flat = y_acc.astype(jnp.bfloat16).reshape(ri_count, -1)
    product = jnp.einsum(
        "pk,qk->pq",
        x_flat,
        lax.all_gather(y_flat, "ri", axis=0, tiled=True),
        preferred_element_type=jnp.float32,
    )
    return lax.psum(product, ("pair", "rep"))


WINDOW = 4 * R + 1
NEAR = 2 * R + 1
TRIM = WINDOW + 1
VBAND = 6 * R + 1
MESH = pl.DeviceIdType.MESH


def remote(src, dst, send, recv, device):
    return pltpu.make_async_remote_copy(
        src_ref=src, dst_ref=dst, send_sem=send, recv_sem=recv, device_id=device, device_id_type=MESH
    )


def fused(
    n, b_ref, gv_ref, go_ref, mask_ref, out_ref,
    three, virtual, occ, present, y_buf, x_buf, sums,
    in_sem, own_sem, right_send, right_recv, left_send, left_recv, f_send, f_recv,
    y_send, y_recv, g_send, g_recv, h_send, h_recv, c_send, c_recv,
):
    z, x, r = lax.axis_index("pair"), lax.axis_index("ri"), lax.axis_index("rep")
    ri_here, nblk, rows, width = b_ref.shape
    nb = gv_ref.shape[0]
    half = go_ref.shape[1]
    reach = nb + 2 * R
    part_rows = rows // 2
    sibling = {"rep": 1 - r}
    partner = {"ri": 1 - x}

    barrier = pltpu.get_barrier_semaphore()
    for d in range(n):
        other = lax.rem(z + d, n)
        if d:
            pl.semaphore_signal(barrier, inc=1, device_id={"pair": other}, device_id_type=MESH)
        pl.semaphore_signal(barrier, inc=1, device_id={"pair": other, "rep": 1 - r}, device_id_type=MESH)
    pl.semaphore_signal(barrier, inc=1, device_id=partner, device_id_type=MESH)

    loads = [
        pltpu.make_async_copy(gv_ref, virtual.at[R : R + nb], in_sem.at[0]),
        pltpu.make_async_copy(go_ref, occ, in_sem.at[1]),
        pltpu.make_async_copy(mask_ref, present, in_sem.at[2]),
    ]
    for load in loads:
        load.start()

    def at_each(step):
        for place in range(n):
            pl.when(z == place)(functools.partial(step, place))

    def needed(place):
        low, high = place * nb - R, place * nb + nb + R
        if low < 0:
            return [(0, high), (nblk + low, -low)]
        if high > nblk:
            return [(0, high - nblk), (low, nblk - low)]
        return [(low, high - low)]

    def from_left(place):
        low = max(place * nb - R, R)
        return [(0, R), (low, nblk - low)]

    def from_right(place):
        high = min(place * nb + nb + R, nblk - R)
        return [(0, high), (nblk - R, R)]

    def count(runs):
        return sum(size for _, size in runs)

    core_part = pl.ds(pl.multiple_of(r * part_rows, part_rows), part_rows)

    def own(q, place):
        return [
            pltpu.make_async_copy(b_ref.at[q, pl.ds(a, m)], three.at[q, pl.ds(a, m), place], own_sem.at[q])
            for a, m in needed(place)
        ]

    def send(q, hop, place):
        for source, to, runs, sems in (
            (place - hop, place + 1, from_left, (right_send, right_recv)),
            (place + hop, place - 1, from_right, (left_send, left_recv)),
        ):
            if 0 <= source < n and 0 <= to < n:
                for a, m in runs(to):
                    dst = three.at[q, pl.ds(a, m), source, core_part]
                    src = b_ref.at[q, pl.ds(a, m), core_part] if hop == 0 else dst
                    remote(src, dst, sems[0].at[q, hop], sems[1].at[q, hop], {"pair": to}).start()

    def sent(q, hop, place):
        for source, to, runs, sems in (
            (place - hop, place + 1, from_left, (right_send, right_recv)),
            (place + hop, place - 1, from_right, (left_send, left_recv)),
        ):
            if 0 <= source < n and 0 <= to < n:
                ref = three.at[q, pl.ds(0, count(runs(to))), source, core_part]
                remote(ref, ref, sems[0].at[q, hop], sems[1].at[q, hop], sibling).wait_send()

    def arrived(q, hop, place):
        for source, runs, sems in (
            (place - 1 - hop, from_left, (right_send, right_recv)),
            (place + 1 + hop, from_right, (left_send, left_recv)),
        ):
            if 0 <= source < n:
                ref = three.at[q, pl.ds(0, count(runs(place))), source, core_part]
                remote(ref, ref, sems[0].at[q, hop], sems[1].at[q, hop], sibling).wait_recv()

    def share(q, hop, place):
        for source in (place - 1 - hop, place + 1 + hop):
            if 0 <= source < n:
                for a, m in needed(place):
                    ref = three.at[q, pl.ds(a, m), source, core_part]
                    remote(ref, ref, f_send.at[q], f_recv.at[q], sibling).start()

    def first_sends(place):
        for q in range(ri_here):
            for copy in own(q, place):
                copy.start()

    pl.semaphore_wait(barrier, 2 * n)
    at_each(functools.partial(send, 0, 0))
    at_each(functools.partial(send, 1, 0))
    at_each(first_sends)

    core_rows = pl.ds(pl.multiple_of(r * half, half), half)
    wide, narrow = TRIM * BS, WINDOW * BS
    last = VBAND * BS
    up, down = {"pair": lax.rem(z + 1, n)}, {"pair": lax.rem(z + n - 1, n)}
    halos = [
        (gv_ref.at[nb - R : nb, core_rows, last - wide : last], virtual.at[0:R, core_rows, last - wide : last], up),
        (gv_ref.at[0:R, core_rows, 0:wide], virtual.at[nb + R : reach, core_rows, 0:wide], down),
    ]

    def block_of(j):
        return lax.rem(z * nb + (nblk - R + j), nblk)

    def occupied(q):
        for i in range(nb):
            parts = []
            for o in range(NEAR):
                block = block_of(i + o)
                part = jnp.dot(
                    occ[i, :, o * BS : (o + 1) * BS], three[q, block].reshape(n * rows, width),
                    preferred_element_type=jnp.float32,
                )
                parts.append([
                    part[:, p * BS : (p + 1) * BS] * present[p, block].astype(jnp.float32) for p in range(NEAR)
                ])
            for t in range(WINDOW):
                total = None
                for o in range(NEAR):
                    if 0 <= t - o < NEAR:
                        part = parts[o][t - o]
                        total = part if total is None else total + part
                y_buf[0, i, q, :, t * BS : (t + 1) * BS] = total.astype(jnp.bfloat16)
        remote(y_buf.at[0, :, q], y_buf.at[1, :, q], y_send.at[q], y_recv.at[q], partner).start()

    for load in loads:
        load.wait()
    def pass_on(q, hop, place):
        arrived(q, hop, place)
        if hop + 1 < n - 1:
            send(q, hop + 1, place)
        if hop == 0 and q + 2 < ri_here:
            send(q + 2, 0, place)
        share(q, hop, place)

    def response(q):
        own_ref = three.at[q, pl.ds(0, reach), 0]
        pltpu.make_async_copy(own_ref, own_ref, own_sem.at[q]).wait()
        shared = three.at[q, pl.ds(0, reach), pl.ds(0, n - 1), core_part]
        remote(shared, shared, f_send.at[q], f_recv.at[q], sibling).wait_recv()
        occupied(q)

    seen = set()

    def visit(q, hop):
        if (q, hop) not in seen and q < ri_here and hop < n - 1:
            seen.add((q, hop))
            at_each(functools.partial(pass_on, q, hop))

    for q in range(ri_here):
        for hop in range(n - 1):
            if hop == n - 2:
                visit(q + 1, 0)
                if q == ri_here - 1:
                    for s, (src, dst, device) in enumerate(halos):
                        remote(src, dst, g_send.at[s], g_recv.at[s], device).start()
            visit(q, hop)
        response(q)

    for s, (src, dst, device) in enumerate(halos):
        remote(dst, dst, g_send.at[s], g_recv.at[s], sibling).wait_recv()
        remote(dst, dst, h_send.at[s], h_recv.at[s], sibling).start()
    for s, (src, dst, device) in enumerate(halos):
        remote(dst, dst, h_send.at[s], h_recv.at[s], sibling).wait_recv()

    def products(side):
        total = None
        for i in range(nb):
            part = lax.dot_general(
                x_buf[i], y_buf[side, i].reshape(ri_here * half, WINDOW * BS),
                (((1,), (1,)), ((), ())), preferred_element_type=jnp.float32,
            )
            total = part if total is None else total + part
        return total

    owners = half // rows
    for i in range(nb):
        total = None
        block = z * nb + i
        for o in range(NEAR):
            left = three[:, block, pl.ds(r * owners, owners), :, o * BS : (o + 1) * BS].reshape(ri_here * half, BS)
            part = jnp.dot(
                left, virtual[i + o, :, (2 * R - o) * BS : (6 * R - o + 1) * BS],
                preferred_element_type=jnp.float32,
            ) * present[o, block].astype(jnp.float32)
            total = part if total is None else total + part
        x_buf[i] = total.astype(jnp.bfloat16)

    size = ri_here * half
    row_id = lax.broadcasted_iota(jnp.int32, (size, size), 0)
    col_id = lax.broadcasted_iota(jnp.int32, (size, size), 1)
    same = lax.rem(row_id, half) == lax.rem(col_id, half)
    col_of = lax.broadcasted_iota(jnp.int32, (ri_here, size), 1) // half
    lane = lax.broadcasted_iota(jnp.int32, (ri_here, BS), 1)
    result = jnp.zeros((ri_here, BS), jnp.float32)
    for side in range(2):
        if side:
            for q in range(ri_here):
                landed = y_buf.at[1, :, q]
                remote(landed, landed, y_send.at[q], y_recv.at[q], partner).wait_recv()
        diagonal = jnp.where(same, products(side), 0.0).reshape(ri_here, half, size).sum(axis=1)
        base = ri_here * (x if side == 0 else 1 - x)
        for q in range(ri_here):
            value = jnp.sum(jnp.where(col_of == q, diagonal, 0.0), axis=1, keepdims=True)
            result = jnp.where(lane == base + q, value, result)

    slot = 2 * z + r
    sums[slot, 0:ri_here, :] = result
    for d in range(n):
        other = lax.rem(z + d, n)
        if d:
            remote(sums.at[slot], sums.at[slot], c_send, c_recv, {"pair": other}).start()
        remote(sums.at[slot], sums.at[slot], c_send, c_recv, {"pair": other, "rep": 1 - r}).start()
    seven = sums.at[0 : 2 * n - 1]
    remote(seven, seven, c_send, c_recv, sibling).wait_recv()
    total = sums[0]
    for s in range(1, 2 * n):
        total = total + sums[s]
    out_ref[...] = total[0:ri_here, 0 : 2 * ri_here]

    remote(seven, seven, c_send, c_recv, sibling).wait_send()
    for q in range(ri_here):
        for hop in range(n - 1):
            at_each(functools.partial(sent, q, hop))
        shared = three.at[q, pl.ds(0, reach), pl.ds(0, n - 1), core_part]
        remote(shared, shared, f_send.at[q], f_recv.at[q], sibling).wait_send()
        remote(y_buf.at[0, :, q], y_buf.at[0, :, q], y_send.at[q], y_recv.at[q], partner).wait_send()
    for s, (src, dst, device) in enumerate(halos):
        remote(src, dst, g_send.at[s], g_recv.at[s], device).wait_send()
        remote(dst, dst, h_send.at[s], h_recv.at[s], sibling).wait_send()


def one_kernel(b_int, gv_band, go_band, mask):
    n = lax.axis_size("pair")
    ri_here, nblk, rows, width = b_int.shape
    nb = gv_band.shape[0]
    half = go_band.shape[1]
    dma = pltpu.SemaphoreType.DMA
    hbm = pl.BlockSpec(memory_space=pltpu.HBM)
    per_hop, per_q = dma((ri_here, n - 1)), dma((ri_here,))
    return pl.pallas_call(
        functools.partial(fused, n),
        out_shape=jax.ShapeDtypeStruct((ri_here, 2 * ri_here), jnp.float32),
        in_specs=[hbm, hbm, hbm, hbm],
        out_specs=pl.BlockSpec(memory_space=pltpu.VMEM),
        scratch_shapes=[
            pltpu.VMEM((ri_here, nblk, n, rows, width), jnp.bfloat16),
            pltpu.VMEM((nb + 2 * R, BS, gv_band.shape[2]), jnp.bfloat16),
            pltpu.VMEM(go_band.shape, jnp.bfloat16),
            pltpu.SMEM(mask.shape[::-1], jnp.int32),
            pltpu.VMEM((2, nb, ri_here, half, WINDOW * BS), jnp.bfloat16),
            pltpu.VMEM((nb, ri_here * half, WINDOW * BS), jnp.bfloat16),
            pltpu.VMEM((2 * n, 8, BS), jnp.float32),
            dma((3,)), per_q, per_hop, per_hop, per_hop, per_hop, per_q, per_q,
            per_q, per_q, dma((2,)), dma((2,)), dma((2,)), dma((2,)), dma, dma,
        ],
        compiler_params=pltpu.CompilerParams(
            collective_id=0, has_side_effects=True, vmem_limit_bytes=63 * 1024 * 1024
        ),
    )(b_int, gv_band, go_band, mask.T)


def on_device(b_int, gv_band, go_band, mask):
    fits = (
        lax.axis_size("ri") == 2
        and lax.axis_size("rep") == 2
        and 2 <= lax.axis_size("pair") <= 4
        and b_int.shape[2] % 32 == 0
        and go_band.shape[1] % b_int.shape[2] == 0
        and b_int.shape[0] in (2, 4, 8)
        and gv_band.shape[0] >= R
        and gv_band.shape[0] + 2 * R <= b_int.shape[1]
    )
    return (one_kernel if fits else per_device)(b_int, gv_band, go_band, mask)


def solution(mesh):
    in_specs = (
        P(("groups", "ri"), None, "pair", None),
        P(("groups", "pair"), None, None),
        P(("groups", "pair"), "rep", None),
        P("groups", None),
    )
    out_specs = P(("groups", "ri"), None)
    return jax.shard_map(
        on_device, mesh=mesh, in_specs=in_specs, out_specs=out_specs, check_vma=False
    )
```

time: 95.9 us -> 74.9 us (0.78)
  Pallas kernels: 90.5 us -> 73.5 us
  local copies, waits for them, and re-layouts: 5.15 us -> 1.26 us
    pallas_call x1, Pallas kernels: 90.5 us -> 73.5 us  [one_kernel(): pl.pallas_call(functools.partial(fused, n), out_shape=jax.ShapeDtypeStruc...]
    unnamed x8 -> x1, local copies, waits for them, and re-layouts: 5.15 us -> 1.26 us
where the time goes in v2:
time: 74.9 us; the launch traced here: 74.8 us
  Pallas kernels  73.5 us (98%)
  local copies, waits for them, and re-layouts  1.26 us (2%)
    pallas_call x1, Pallas kernels, one_kernel(): pl.pallas_call(functools.partial(fused, n), out_shape=jax.ShapeDtypeStruc...  73.5 us

profile of v2, /device:TPU:0, one launch (start us, length us, event | category | flops | bytes accessed | tf_op | source)
XLA Modules:
  0.0 74.8 jit_solution(1248728289172652577)
XLA Ops:
  0.0 73.5 %shard_map.46 = f32[4,8]{1,0:T(4,128)} custom-call(bf16[4,12,32,640]{3,2,1,0:T(8,128)(2,1)} %b_ref.1, bf16[3,128,1664]{2,1,0:T(8,128)(2,1)} %gv_ref.1, bf16[3,64,640]{2,1,0:T(8,128)(2,1)} %go_ref.1, s32[5,12]{1,0:T(8,128)} %bitcast.1), custom_call_target="tpu_custom_call" | custom-call | tf_op jit(solution)/shard_map/pallas_call | solution.py:343
  73.5 1.3 %copy.6 = f32[4,8]{1,0:T(4,128)} copy(f32[4,8]{1,0:T(4,128)} %shard_map.46) | data formatting | bytes 256

commit v3 on v2

--- a/solution.py
+++ b/solution.py
@@ -86,7 +86,7 @@
 
 def fused(
     n, b_ref, gv_ref, go_ref, mask_ref, out_ref,
-    three, virtual, occ, present, y_buf, x_buf, sums,
+    three, virtual, occ, present, y_buf, x_acc, x_buf, sums,
     in_sem, own_sem, right_send, right_recv, left_send, left_recv, f_send, f_recv,
     y_send, y_recv, g_send, g_recv, h_send, h_recv, c_send, c_recv,
 ):
@@ -223,7 +223,7 @@
                         part = parts[o][t - o]
                         total = part if total is None else total + part
                 y_buf[0, i, q, :, t * BS : (t + 1) * BS] = total.astype(jnp.bfloat16)
-        remote(y_buf.at[0, :, q], y_buf.at[1, :, q], y_send.at[q], y_recv.at[q], partner).start()
+            remote(y_buf.at[0, i, q], y_buf.at[1, i, q], y_send.at[q], y_recv.at[q], partner).start()
 
     for load in loads:
         load.wait()
@@ -259,6 +259,26 @@
             visit(q, hop)
         response(q)
 
+    owners = half // rows
+
+    def virtual_products(i, offsets):
+        total = None
+        block = z * nb + i
+        for o in offsets:
+            left = three[:, block, pl.ds(r * owners, owners), :, o * BS : (o + 1) * BS].reshape(ri_here * half, BS)
+            part = jnp.dot(
+                left, virtual[i + o, :, (2 * R - o) * BS : (6 * R - o + 1) * BS],
+                preferred_element_type=jnp.float32,
+            ) * present[o, block].astype(jnp.float32)
+            total = part if total is None else total + part
+        return total
+
+    def here(i, o):
+        return R <= i + o < R + nb
+
+    for i in range(nb):
+        x_acc[i] = virtual_products(i, [o for o in range(NEAR) if here(i, o)])
+
     for s, (src, dst, device) in enumerate(halos):
         remote(dst, dst, g_send.at[s], g_recv.at[s], sibling).wait_recv()
         remote(dst, dst, h_send.at[s], h_recv.at[s], sibling).start()
@@ -275,17 +295,10 @@
             total = part if total is None else total + part
         return total
 
-    owners = half // rows
     for i in range(nb):
-        total = None
-        block = z * nb + i
-        for o in range(NEAR):
-            left = three[:, block, pl.ds(r * owners, owners), :, o * BS : (o + 1) * BS].reshape(ri_here * half, BS)
-            part = jnp.dot(
-                left, virtual[i + o, :, (2 * R - o) * BS : (6 * R - o + 1) * BS],
-                preferred_element_type=jnp.float32,
-            ) * present[o, block].astype(jnp.float32)
-            total = part if total is None else total + part
+        total = x_acc[i]
+        if not all(here(i, o) for o in range(NEAR)):
+            total = total + virtual_products(i, [o for o in range(NEAR) if not here(i, o)])
         x_buf[i] = total.astype(jnp.bfloat16)
 
     size = ri_here * half
@@ -351,6 +364,7 @@
             pltpu.VMEM(go_band.shape, jnp.bfloat16),
             pltpu.SMEM(mask.shape[::-1], jnp.int32),
             pltpu.VMEM((2, nb, ri_here, half, WINDOW * BS), jnp.bfloat16),
+            pltpu.VMEM((nb, ri_here * half, WINDOW * BS), jnp.float32),
             pltpu.VMEM((nb, ri_here * half, WINDOW * BS), jnp.bfloat16),
             pltpu.VMEM((2 * n, 8, BS), jnp.float32),
             dma((3,)), per_q, per_hop, per_hop, per_hop, per_hop, per_q, per_q,

time: 74.9 us -> 74.3 us (level)
  no operation moved by 1% of the time
where the time goes in v3:
time: 74.3 us; the launch traced here: 74.2 us
  Pallas kernels  72.9 us (98%)
  local copies, waits for them, and re-layouts  1.26 us (2%)
    pallas_call x1, Pallas kernels, one_kernel(): pl.pallas_call(functools.partial(fused, n), out_shape=jax.ShapeDtypeStruc...  72.9 us

profile of v3, /device:TPU:0, one launch (start us, length us, event | category | flops | bytes accessed | tf_op | source)
XLA Modules:
  0.0 74.2 jit_solution(1738230922738815472)
XLA Ops:
  0.0 72.9 %shard_map.46 = f32[4,8]{1,0:T(4,128)} custom-call(bf16[4,12,32,640]{3,2,1,0:T(8,128)(2,1)} %b_ref.1, bf16[3,128,1664]{2,1,0:T(8,128)(2,1)} %gv_ref.1, bf16[3,64,640]{2,1,0:T(8,128)(2,1)} %go_ref.1, s32[5,12]{1,0:T(8,128)} %bitcast.1), custom_call_target="tpu_custom_call" | custom-call | tf_op jit(solution)/shard_map/pallas_call | solution.py:356
  72.9 1.3 %copy.6 = f32[4,8]{1,0:T(4,128)} copy(f32[4,8]{1,0:T(4,128)} %shard_map.46) | data formatting | bytes 256
